TPU v7x, 32 devices: a whole 2x2x4 slice. The times are simulated.
32 devices in a mesh: rep: 4 (over y, x), shard: 8 (over z, core).
Axes of the slice: x: 2, y: 2, z: 4, core: 2. Of those that a mesh axis runs over, the one named last changes fastest.
Arguments:
- features: bfloat16 [16384, 1024], P(('rep', 'shard')), may hold values from -6 to 6
- cotangent: bfloat16 [16384, 1024], P(('rep', 'shard')), may hold values from -6 to 6
- cross_weight: bfloat16 [1024, 1024], replicated, may hold values from -0.1875 to 0.1875
- cross_bias: float32 [1024], replicated, may hold values from -3 to 3
- emb_table: float32 [32768, 128], P('shard'), may hold values from -6 to 6
- row_accum: float32 [32768], P('shard'), may hold values from 0.5 to 50
- send_bags: int32 [32, 8, 256], P(('rep', 'shard')), may hold values from 0 to 3583, as said below
- slot_counts: int32 [32, 8], P(('rep', 'shard')), may hold values from 64 to 256, as said below
- recv_rows: int32 [32, 8, 256], P(('rep', 'shard')), may hold values from 0 to 4095, as said below
- touched_rows: int32 [8, 512], P('shard'), may hold values from 0 to 4095, as said below
Outputs:
- weight_grad: float32 [1024, 1024], replicated
- bias_grad: float32 [1024], replicated
- dense_grad: bfloat16 [16384, 128], P(('rep', 'shard'))
- new_table: float32 [32768, 128], P('shard')
- new_accum: float32 [32768], P('shard')
Inputs may be any that keep to these rules, and one draw needn't show every extreme that they name: `send_bags`: bag b * 7 + f of a device is feature f of its sample b. The first slot_counts[d, s] slots of a block are live; in each replica group some shard receives 256 live slots from every device of the group. `recv_rows`: every slot, live or not, names a row listed in touched_rows for the owner's shard. `touched_rows`: ascending and distinct.
All inputs are finite; a program needn't handle non-finite values.
Results may differ from a plain program's by a relative error of at most 0.0055.
Values may be sent and summed in bfloat16 or wider, within the bound.
A program may use at most 128 MiB of HBM per device.

v0:
```python
import math

import jax
import jax.numpy as jnp
from jax import lax
from jax.sharding import PartitionSpec as P

learn_rate = 0.5
keep_rate = 0.9


def adagrad_rows(table_rows, accum_rows, grads):
    new_accum = accum_rows + jnp.mean(grads * grads, axis=1)
    new_rows = keep_rate * table_rows - learn_rate * grads / jnp.sqrt(new_accum)[:, None]
    return (new_rows, new_accum)


def blocked(count, fn):
    step_rows = math.gcd(count, 512)
    index_blocks = jnp.arange(count, dtype=jnp.int32).reshape(-1, step_rows)
    result = lax.map(fn, index_blocks)
    return result.reshape((count,) + result.shape[2:])


def per_device(
    features,
    cotangent,
    cross_weight,
    cross_bias,
    emb_table,
    row_accum,
    send_bags,
    slot_counts,
    recv_rows,
    touched_rows,
):
    width = emb_table.shape[1]
    shard_rows = emb_table.shape[0]
    total_tokens = features.shape[0] * lax.axis_size("rep") * lax.axis_size("shard")
    scale = 1.0 / jnp.sqrt(jnp.float32(total_tokens))
    linear = jnp.dot(features, cross_weight, preferred_element_type=jnp.float32) + cross_bias
    cot_f = cotangent.astype(jnp.float32)
    gated = (cot_f * features.astype(jnp.float32)).astype(jnp.bfloat16)
    weight_part = lax.dot_general(
        features, gated, (((0,), (0,)), ((), ())), preferred_element_type=jnp.float32
    )
    bias_part = jnp.sum(gated.astype(jnp.float32), axis=0)
    backprop = lax.dot_general(
        gated, cross_weight, (((1,), (1,)), ((), ())), preferred_element_type=jnp.float32
    )
    input_grad = cot_f * linear + backprop + cot_f
    dense_grad = input_grad[:, :width].astype(jnp.bfloat16)
    pooled = input_grad[:, width:].astype(jnp.bfloat16).reshape(-1, width)
    bag_ids = send_bags[0]
    shard_count = bag_ids.shape[0]
    slot_total = bag_ids.shape[1]
    live_mask = jnp.arange(slot_total, dtype=jnp.int32)[None, :] < slot_counts[0][:, None]
    flat_bags = jnp.where(live_mask, bag_ids, -1).reshape(-1)
    bag_range = jnp.arange(pooled.shape[0], dtype=jnp.int32)

    def pick_bags(positions):
        select = (flat_bags[positions][:, None] == bag_range[None, :]).astype(jnp.bfloat16)
        return jnp.dot(select, pooled, preferred_element_type=jnp.float32).astype(jnp.bfloat16)

    outgoing = blocked(shard_count * slot_total, pick_bags).reshape(shard_count, slot_total, width)
    incoming = lax.all_to_all(outgoing, "shard", split_axis=0, concat_axis=0, tiled=True)
    weight_sum, bias_sum = lax.psum((weight_part, bias_part), ("rep", "shard"))
    weight_grad = weight_sum * scale
    bias_grad = bias_sum * scale
    incoming_rows = incoming.reshape(-1, width)
    slot_rows = recv_rows[0].reshape(-1)
    touched = touched_rows[0]
    row_range = jnp.arange(shard_rows, dtype=jnp.int32)
    marks = jnp.any(row_range[:, None] == touched[None, :], axis=1)

    def row_block(row_ids):
        select = (row_ids[:, None] == slot_rows[None, :]).astype(jnp.bfloat16)
        return jnp.dot(select, incoming_rows, preferred_element_type=jnp.float32)

    local_sums = blocked(shard_rows, row_block)
    row_grads = lax.psum(local_sums.astype(jnp.bfloat16), "rep").astype(jnp.float32)
    upd_table, upd_accum = adagrad_rows(emb_table, row_accum, row_grads)
    new_table = jnp.where(marks[:, None], upd_table, emb_table)
    new_accum = jnp.where(marks, upd_accum, row_accum)
    return (weight_grad, bias_grad, dense_grad, new_table, new_accum)


def solution(mesh):
    in_specs = (
        P(("rep", "shard"), None),
        P(("rep", "shard"), None),
        P(),
        P(),
        P("shard", None),
        P("shard"),
        P(("rep", "shard"), None, None),
        P(("rep", "shard"), None),
        P(("rep", "shard"), None, None),
        P("shard", None),
    )
    out_specs = (P(), P(), P(("rep", "shard"), None), P("shard", None), P("shard"))
    return jax.shard_map(
        per_device, mesh=mesh, in_specs=in_specs, out_specs=out_specs, check_vma=False
    )
```

profile of v0, /device:TPU:0, one launch (start us, length us, event | category | flops | bytes accessed | tf_op | source)
XLA Modules:
  0.0 301.9 jit_solution(12534788017708602025)
XLA Ops:
  8.8 2.6 fusion.29
  14.9 2.7 reshape.80
  17.7 25.5 %while.22 = (s32[]{:T(128)}, bf16[4,512,128]{2,1,0:T(8,128)(2,1)}, s32[4,512]{1,0:T(4,128)S(1)}, s32[2048]{0:T(1024)S(1)}, bf16[3584,128]{1,0:T(8,128)(2,1)}, /*index=5*/s32[]{:T(128)}) while((s32[]{:T(128)}, bf16[4,512,128]{2,1,0:T(8,128)(2,1)}, s32[4,512]{1,0:T(4,128)S(1)}, s32[2048]{0:T(1024)S(1)}, bf16[3584,128]{1,0:T(8,128)(2,1)}, ...), condition=%wide.region_5.6_spmd.clone, body=%wide.region_4.5_spmd.clone.sunk | while | flops 471665152 | bytes 1067093 | solution.py:21
  17.7 3.1 %gather_fusion = s32[512]{0:T(512)S(1)} fusion(s32[2048]{0:T(1024)S(1)} %get-tuple-element.192, s32[1024]{0:T(1024)S(1)} %pad_clamp_fusion.2), kind=kCustom, calls=%fused_computation.clone.clone.1 | custom fusion | bytes 6144 | tf_op jit(solution)/shard_map/while/body/eval_jaxpr/gather | solution.py:62
  20.9 3.2 %fusion.45 = bf16[4,512,128]{2,1,0:T(8,128)(2,1)} fusion(bf16[4,512,128]{2,1,0:T(8,128)(2,1)} %get-tuple-element.184, s32[]{:T(128)S(6)} %copy.27, bf16[3584,128]{1,0:T(8,128)(2,1)} %get-tuple-element.193, s32[512]{0:T(512)S(1)} %gather_fusion), kind=kOutput, calls=%fused_computation.14.clone.1 | convolution fusion | flops 471662592 | bytes 1050628 | tf_op jit(solution)/shard_map/while/body/eval_jaxpr/dot_general | solution.py:63
  24.1 3.1 %gather_fusion = s32[512]{0:T(512)S(1)} fusion(s32[2048]{0:T(1024)S(1)} %get-tuple-element.192, s32[1024]{0:T(1024)S(1)} %pad_clamp_fusion.2), kind=kCustom, calls=%fused_computation.clone.clone.1 | custom fusion | bytes 6144 | tf_op jit(solution)/shard_map/while/body/eval_jaxpr/gather | solution.py:62
  27.2 3.2 %fusion.45 = bf16[4,512,128]{2,1,0:T(8,128)(2,1)} fusion(bf16[4,512,128]{2,1,0:T(8,128)(2,1)} %get-tuple-element.184, s32[]{:T(128)S(6)} %copy.27, bf16[3584,128]{1,0:T(8,128)(2,1)} %get-tuple-element.193, s32[512]{0:T(512)S(1)} %gather_fusion), kind=kOutput, calls=%fused_computation.14.clone.1 | convolution fusion | flops 471662592 | bytes 1050628 | tf_op jit(solution)/shard_map/while/body/eval_jaxpr/dot_general | solution.py:63
  30.5 3.1 %gather_fusion = s32[512]{0:T(512)S(1)} fusion(s32[2048]{0:T(1024)S(1)} %get-tuple-element.192, s32[1024]{0:T(1024)S(1)} %pad_clamp_fusion.2), kind=kCustom, calls=%fused_computation.clone.clone.1 | custom fusion | bytes 6144 | tf_op jit(solution)/shard_map/while/body/eval_jaxpr/gather | solution.py:62
  33.6 3.2 %fusion.45 = bf16[4,512,128]{2,1,0:T(8,128)(2,1)} fusion(bf16[4,512,128]{2,1,0:T(8,128)(2,1)} %get-tuple-element.184, s32[]{:T(128)S(6)} %copy.27, bf16[3584,128]{1,0:T(8,128)(2,1)} %get-tuple-element.193, s32[512]{0:T(512)S(1)} %gather_fusion), kind=kOutput, calls=%fused_computation.14.clone.1 | convolution fusion | flops 471662592 | bytes 1050628 | tf_op jit(solution)/shard_map/while/body/eval_jaxpr/dot_general | solution.py:63
  36.8 3.1 %gather_fusion = s32[512]{0:T(512)S(1)} fusion(s32[2048]{0:T(1024)S(1)} %get-tuple-element.192, s32[1024]{0:T(1024)S(1)} %pad_clamp_fusion.2), kind=kCustom, calls=%fused_computation.clone.clone.1 | custom fusion | bytes 6144 | tf_op jit(solution)/shard_map/while/body/eval_jaxpr/gather | solution.py:62
  40.0 3.2 %fusion.45 = bf16[4,512,128]{2,1,0:T(8,128)(2,1)} fusion(bf16[4,512,128]{2,1,0:T(8,128)(2,1)} %get-tuple-element.184, s32[]{:T(128)S(6)} %copy.27, bf16[3584,128]{1,0:T(8,128)(2,1)} %get-tuple-element.193, s32[512]{0:T(512)S(1)} %gather_fusion), kind=kOutput, calls=%fused_computation.14.clone.1 | convolution fusion | flops 471662592 | bytes 1050628 | tf_op jit(solution)/shard_map/while/body/eval_jaxpr/dot_general | solution.py:63
  43.2 6.3 %all-to-all-start = ((bf16[8,256,128]{2,1,0:T(8,128)(2,1)}), bf16[8,256,128]{2,1,0:T(8,128)(2,1)}, u32[]{:S(2)}, u32[]{:S(2)}) async-start(bf16[8,256,128]{2,1,0:T(8,128)(2,1)} %bitcast.48), calls=%async_computation | async-start | bytes 1048576 | tf_op jit(solution)/shard_map/all_to_all | solution.py:66
  49.6 15.4 %all-to-all-done = bf16[8,256,128]{2,1,0:T(8,128)(2,1)} async-done(((bf16[8,256,128]{2,1,0:T(8,128)(2,1)}), bf16[8,256,128]{2,1,0:T(8,128)(2,1)}, u32[]{:S(2)}, u32[]{:S(2)}) %all-to-all-start) | async-done | bytes 524320 | tf_op jit(solution)/shard_map/all_to_all | solution.py:66
  65.0 19.9 %while.21 = (s32[]{:T(128)}, bf16[8,512,128]{2,1,0:T(8,128)(2,1)}, s32[8,512]{1,0:T(8,128)S(1)}, s32[1,8,256]{2,1,0:T(8,128)S(1)}, bf16[2048,128]{1,0:T(8,128)(2,1)}, /*index=5*/s32[]{:T(128)}) while((s32[]{:T(128)}, bf16[8,512,128]{2,1,0:T(8,128)(2,1)}, s32[8,512]{1,0:T(8,128)S(1)}, s32[1,8,256]{2,1,0:T(8,128)S(1)}, ...), condition=%wide.region_7.8_spmd, body=%wide.region_6.7_spmd.sunk | while | flops 269484032 | bytes 817237 | solution.py:21
  65.0 2.5 fusion.43
  67.5 2.5 fusion.43
  70.0 2.5 fusion.43
  72.5 2.5 fusion.43
  74.9 2.5 fusion.43
  77.4 2.5 fusion.43
  79.9 2.5 fusion.43
  82.4 2.5 fusion.43
  84.9 4.5 %convolution_bitcast_fusion = f32[1024,1024]{0,1:T(8,128)} fusion(bf16[512,1024]{1,0:T(8,128)(2,1)S(1)} %copy-done.1, bf16[512,1024]{1,0:T(8,128)(2,1)} %param.15), kind=kOutput, calls=%fused_computation.24 | convolution fusion | flops 1075838976 | bytes 6291456 | tf_op jit(solution)/shard_map/dot_general | solution.py:44
  89.5 1.6 slice.12
  91.1 1.6 convert_reduce_fusion
  92.7 37.9 %psum.22 = f32[1024]{0:T(1024)S(1)} all-reduce(f32[1024]{0:T(1024)S(1)} %convert_reduce_fusion), channel_id=1, replica_groups=mesh['rep'=4,'shard'=8] {'rep','shard'}, use_global_device_ids=true, to_apply=%region_2.3 | all-reduce | flops 1024 | bytes 8192 | tf_op jit(solution)/shard_map/psum | solution.py:67
  132.1 4.7 %all-reduce.5.cloned.1.call-done = bf16[4096,128]{1,0:T(8,128)(2,1)} async-done(((bf16[4096,128]{1,0:T(8,128)(2,1)}), bf16[4096,128]{1,0:T(8,128)(2,1)}) %all-reduce.5.cloned.1.call-update) | async-done | bytes 1048592 | tf_op jit(solution)/shard_map/psum | solution.py:81
  136.8 1.8 fusion.21
  139.3 4.5 %fusion.20 = f32[4096,128]{1,0:T(8,128)} fusion(f32[4096,128]{1,0:T(8,128)} %param.18, bf16[4096,128]{1,0:T(8,128)(2,1)} %all-reduce.5.cloned.1.call-done, f32[4096]{0:T(1024)S(1)} %get-tuple-element.114, pred[4096]{0:T(1024)(128)(4,1)S(1)} %fusion.17), kind=kLoop, calls=%fused_computation.27 | loop fusion | flops 3145728 | bytes 5263360 | tf_op jit(solution)/shard_map/jit(_where)/select_n | solution.py:83
  143.8 140.9 %all-reduce.3.cloned.1.call-done = f32[1024,1024]{0,1:T(8,128)} async-done(((f32[1024,1024]{0,1:T(8,128)}), f32[1024,1024]{0,1:T(8,128)}) %all-reduce.3.cloned.1.call-update) | async-done | bytes 4194320 | tf_op jit(solution)/shard_map/psum | solution.py:67
  284.8 5.0 %broadcast_multiply_fusion = f32[1024,1024]{0,1:T(8,128)} fusion(f32[1024,1024]{0,1:T(8,128)} %all-reduce.3.cloned.1.call-done), kind=kLoop, calls=%fused_computation.33 | loop fusion | flops 1048576 | bytes 8388608 | tf_op jit(solution)/shard_map/mul | solution.py:68
  289.7 5.3 %copy.17 = f32[1024,1024]{1,0:T(8,128)} copy(f32[1024,1024]{0,1:T(8,128)} %broadcast_multiply_fusion) | data formatting | bytes 8388608
  (57 shorter events, 7.5 us)
Async XLA Ops:
  7.2 1.6 copy-start
  8.8 2.7 copy-start.1
  8.8 2.7 copy-start.2
  8.8 2.7 copy-start.6
  13.0 1.0 copy-start.3
  17.7 47.3 %copy-start.4 = (s32[1,8,256]{2,1,0:T(8,128)S(1)}, s32[1,8,256]{2,1,0:T(8,128)}, u32[]{:S(2)}) copy-start(s32[1,8,256]{2,1,0:T(8,128)} %param.22) | copy-start | bytes 24580
  43.2 21.8 %all-to-all-start = ((bf16[8,256,128]{2,1,0:T(8,128)(2,1)}), bf16[8,256,128]{2,1,0:T(8,128)(2,1)}, u32[]{:S(2)}, u32[]{:S(2)}) async-start(bf16[8,256,128]{2,1,0:T(8,128)(2,1)} %bitcast.48), calls=%async_computation | async-start | bytes 1048576 | tf_op jit(solution)/shard_map/all_to_all | solution.py:66
  49.5 87.3 %all-reduce.5.cloned.1.call-start = ((), (), s32[]{:S(2)}) async-start(), calls=%async_computation.2 | async-start | bytes 2097152 | tf_op jit(solution)/shard_map/psum | solution.py:81
  84.9 199.9 %all-reduce.3.cloned.1.call-start = ((), (), s32[]{:S(2)}) async-start(), calls=%async_computation.1 | async-start | bytes 8388608 | tf_op jit(solution)/shard_map/psum | solution.py:67
  89.5 41.1 %copy-start.7 = (s32[1,512]{1,0:T(1,128)S(1)}, s32[1,512]{1,0:T(1,128)}, u32[]{:S(2)}) copy-start(s32[1,512]{1,0:T(1,128)} %param.23) | copy-start | bytes 6148
  89.5 49.2 %copy-start.5 = (f32[4096]{0:T(1024)S(1)}, f32[4096]{0:T(1024)}, u32[]{:S(2)}) copy-start(f32[4096]{0:T(1024)} %param.19) | copy-start | bytes 49156
Sparse Core Ops, SparseCore 0:
  85.0 51.8 all-reduce.4
  142.9 141.7 all-reduce.2
where the time goes:
time: 303 us; the launch traced here: 302 us
  waiting for transfers between devices  161 us (53%)
  matrix products  41.2 us (14%)
  blocking collectives  37.9 us (13%)
  local copies, waits for them, and re-layouts  25 us (8%)
  other arithmetic  16 us (5%)
  between operations  14.2 us (5%)
  starting transfers between devices  6.4 us (2%)
    psum x1, waiting for transfers between devices, per_device(): weight_sum, bias_sum = lax.psum((weight_part, bias_part), ('rep', 'shard'))  141 us
    psum x1, blocking collectives, per_device(): weight_sum, bias_sum = lax.psum((weight_part, bias_part), ('rep', 'shard'))  37.9 us
    dot_general x8, matrix products, row_block(): return jnp.dot(select, incoming_rows, preferred_element_type=jnp.float32)  19.7 us
    all_to_all x1, waiting for transfers between devices, per_device(): lax.all_to_all(outgoing, 'shard', split_axis=0, concat_axis=0, tiled=True)  15.4 us
    dot_general x4, matrix products, pick_bags(): jnp.dot(select, pooled, preferred_element_type=jnp.float32)  12.8 us
    gather x4, local copies, waits for them, and re-layouts, pick_bags(): flat_bags[positions][:, None] == bag_range[None, :]  12.6 us
    unnamed x18, local copies, waits for them, and re-layouts  7.05 us
    all_to_all x1, starting transfers between devices, per_device(): lax.all_to_all(outgoing, 'shard', split_axis=0, concat_axis=0, tiled=True)  6.33 us
  transfers between devices with their start and end apart: 3, of which 3 were waited for; matrix products, arithmetic and copies ran while one was open for 5% of the time, Pallas kernels for 0%

commit v1 on v0

v1 whole, which is shorter than its diff:
```python
import functools

import jax
import jax.numpy as jnp
from jax import lax
from jax.experimental import pallas as pl
from jax.experimental.pallas import tpu as pltpu
from jax.sharding import PartitionSpec as P

learn_rate = 0.5
keep_rate = 0.9
MESH = pl.DeviceIdType.MESH
F32 = jnp.float32
BF16 = jnp.bfloat16


def step_kernel(
    n_rep,
    n_shard,
    feat_ref,
    cot_ref,
    w_ref,
    cbias_ref,
    code_ref,
    rows_ref,
    touched_ref,
    wsum_ref,
    bsum_ref,
    dense_ref,
    rowt_ref,
    gated,
    ig,
    wown,
    wsend,
    wpair,
    p1buf,
    p2buf,
    p3buf,
    bbuf1,
    bbuf2,
    bbuf3,
    outgoing,
    incoming,
    rowacc,
    rowsend,
    rowbuf,
    p1_sem,
    p2_sem,
    p3_sem,
    b1_sem,
    b2_sem,
    b3_sem,
    a2a_sem,
    rrs_sem,
    rag_sem,
    agz_sem,
    agr_sem,
    agc_sem,
):
    nz = n_shard // 2
    rep = lax.axis_index("rep")
    shard = lax.axis_index("shard")
    core = lax.rem(shard, 2)
    zi = shard // 2
    partner = zi * 2 + (1 - core)
    tok, d = feat_ref.shape
    width = dense_ref.shape[1]
    feats = d // width - 1
    half = d // 2
    rblk = d // n_rep
    zblk = rblk // nz
    touched_count = rowt_ref.shape[0]
    tblk = touched_count // n_rep
    slots = code_ref.shape[1]

    def rep_peer(o):
        return lax.rem(rep + o, n_rep)

    def rep_from(o):
        return lax.rem(rep + n_rep - o, n_rep)

    def z_peer(o):
        return lax.rem(zi + o, nz)

    def z_from(o):
        return lax.rem(zi + nz - o, nz)

    def shard_peer(o):
        return lax.rem(shard + o, n_shard)

    def shard_from(o):
        return lax.rem(shard + n_shard - o, n_shard)

    def remote(src, dst, sems, index, target):
        return pltpu.make_async_remote_copy(
            src_ref=src,
            dst_ref=dst,
            send_sem=sems.at[0, index],
            recv_sem=sems.at[1, index],
            device_id=target,
            device_id_type=MESH,
        )

    barrier = pltpu.get_barrier_semaphore()
    for o in range(1, n_shard):
        pl.semaphore_signal(
            barrier, inc=1, device_id={"shard": shard_peer(o)}, device_id_type=MESH
        )
    for o in range(1, n_rep):
        pl.semaphore_signal(barrier, inc=1, device_id={"rep": rep_peer(o)}, device_id_type=MESH)

    @pl.loop(0, tok // 128)
    def _(i):
        r = pl.ds(pl.multiple_of(i * 128, 128), 128)
        gated[r, :] = (cot_ref[r, :].astype(F32) * feat_ref[r, :].astype(F32)).astype(BF16)

    def weight_half(col_half, out, out_type):
        cols = pl.ds(pl.multiple_of(col_half * half, half), half)

        @pl.loop(0, d // 256)
        def _(i):
            r = pl.ds(pl.multiple_of(i * 256, 256), 256)
            out[r, :] = lax.dot_general(
                feat_ref[:, r], gated[:, cols], (((0,), (0,)), ((), ())), preferred_element_type=F32
            ).astype(out_type)

    weight_half(1 - core, wsend, BF16)
    pl.semaphore_wait(barrier, n_shard - 1 + n_rep - 1)
    p1 = remote(wsend, p1buf, p1_sem, 0, {"shard": partner})
    p1.start()
    weight_half(core, wown, F32)
    bias_row = jnp.sum(gated[...].astype(F32), axis=0, keepdims=True)
    for j in range(d // 128):
        bbuf1[0, pl.ds(j, 1), :] = bias_row[:, j * 128 : (j + 1) * 128]
    b1 = remote(bbuf1.at[0], bbuf1.at[1], b1_sem, 0, {"shard": partner})
    b1.start()

    p1.wait_recv()

    @pl.loop(0, n_rep)
    def _(i):
        r = pl.ds(pl.multiple_of(i * rblk, rblk), rblk)
        wpair[r, :] = (wown[r, :] + p1buf[r, :].astype(F32)).astype(BF16)

    def p2(o):
        target = rep_peer(o)
        r = pl.ds(pl.multiple_of(target * rblk, rblk), rblk)
        return remote(wpair.at[r, :], p2buf.at[o], p2_sem, o, {"rep": target})

    for o in range(1, n_rep):
        p2(o).start()
    b1.wait_recv()
    bbuf2[rep] = bbuf1[0] + bbuf1[1]

    def b2(o, slot):
        return remote(bbuf2.at[slot], bbuf2.at[slot], b2_sem, o, {"rep": rep_peer(o)})

    for o in range(1, n_rep):
        b2(o, rep).start()

    @pl.loop(0, d // 256)
    def _(i):
        c = pl.ds(pl.multiple_of(i * 256, 256), 256)
        linear = jnp.dot(feat_ref[...], w_ref[:, c], preferred_element_type=F32) + cbias_ref[:, c]
        back = lax.dot_general(
            gated[...], w_ref[c, :], (((1,), (1,)), ((), ())), preferred_element_type=F32
        )
        cot = cot_ref[:, c].astype(F32)
        ig[:, c] = (cot * linear + back + cot).astype(BF16)

    dense_ref[...] = ig[:, :width]

    def gather(dest):
        code = jnp.transpose(jnp.broadcast_to(code_ref[pl.ds(dest, 1), :], (128, slots)))
        sample = jnp.right_shift(code, 3)
        feature = jnp.bitwise_and(code, 7)
        lane = lax.broadcasted_iota(jnp.int32, (slots, 128), 1)
        select = jnp.concatenate(
            [jnp.where(sample == lane + k * 128, 1.0, 0.0) for k in range(tok // 128)], axis=1
        ).astype(BF16)
        wide = jnp.dot(select, ig[:, width:], preferred_element_type=F32)
        picked = jnp.zeros((slots, width), F32)
        for f in range(feats):
            picked = jnp.where(feature == f, wide[:, f * width : (f + 1) * width], picked)
        return picked.astype(BF16)

    def a2a(o):
        dest = shard_peer(o)
        return remote(outgoing.at[dest], incoming.at[shard], a2a_sem, o, {"shard": dest})

    def a2a_in(o):
        src = shard_from(o)
        return remote(outgoing.at[src], incoming.at[src], a2a_sem, o, {"shard": src})

    @pl.loop(1, n_shard)
    def _(o):
        outgoing[shard_peer(o)] = gather(shard_peer(o))
        a2a(o).start()

    incoming[shard] = gather(shard)

    for o in range(1, n_rep):
        p2(o).wait_recv()
    own_rows = pl.ds(pl.multiple_of(rep * rblk, rblk), rblk)
    total = wpair[own_rows, :].astype(F32)
    for o in range(1, n_rep):
        total = total + p2buf[o].astype(F32)
    p2buf[0] = total.astype(BF16)

    def p3(o):
        target = z_peer(o)
        r = pl.ds(pl.multiple_of(target * zblk, zblk), zblk)
        return remote(p2buf.at[0, r, :], p3buf.at[o], p3_sem, o, {"shard": target * 2 + core})

    for o in range(1, nz):
        p3(o).start()
    for o in range(1, n_rep):
        b2(o, rep_from(o)).wait_recv()
    bias_rep = bbuf2[0]
    for q in range(1, n_rep):
        bias_rep = bias_rep + bbuf2[q]
    bbuf3[zi] = bias_rep

    def b3(o, slot):
        return remote(
            bbuf3.at[slot], bbuf3.at[slot], b3_sem, o, {"shard": z_peer(o) * 2 + core}
        )

    for o in range(1, nz):
        b3(o, zi).start()

    def add_source(src):
        select = jnp.where(touched_ref[...] == rows_ref[pl.ds(src, 1), :], 1.0, 0.0).astype(BF16)
        return jnp.dot(select, incoming[src], preferred_element_type=F32)

    rowacc[...] = add_source(shard)

    @pl.loop(1, n_shard)
    def _(o):
        a2a_in(o).wait_recv()
        rowacc[...] += add_source(shard_from(o))

    rowsend[...] = rowacc[...].astype(BF16)

    def rrs(o):
        target = rep_peer(o)
        r = pl.ds(pl.multiple_of(target * tblk, tblk), tblk)
        return remote(rowsend.at[r, :], rowbuf.at[o], rrs_sem, o, {"rep": target})

    for o in range(1, n_rep):
        rrs(o).start()

    for o in range(1, nz):
        p3(o).wait_recv()
    own_part = p2buf[0, pl.ds(pl.multiple_of(zi * zblk, zblk), zblk), :].astype(F32)
    for o in range(1, nz):
        own_part = own_part + p3buf[o].astype(F32)
    own_cols = pl.ds(pl.multiple_of(core * half, half), half)
    other_cols = pl.ds(pl.multiple_of((1 - core) * half, half), half)

    def z_rows(z):
        return pl.ds(pl.multiple_of(rep * rblk + z * zblk, zblk), zblk)

    wsum_ref[z_rows(zi), own_cols] = own_part.astype(BF16)

    def agz(o, z):
        place = wsum_ref.at[z_rows(z), own_cols]
        return remote(place, place, agz_sem, o, {"shard": z_peer(o) * 2 + core})

    for o in range(1, nz):
        agz(o, zi).start()

    for o in range(1, n_rep):
        rrs(o).wait_recv()
    mine = pl.ds(pl.multiple_of(rep * tblk, tblk), tblk)
    row_total = rowacc[mine, :]
    for o in range(1, n_rep):
        row_total = row_total + rowbuf[o].astype(F32)
    rowt_ref[mine, :] = row_total.astype(BF16)

    def rag(o, q):
        place = rowt_ref.at[pl.ds(pl.multiple_of(q * tblk, tblk), tblk), :]
        return remote(place, place, rag_sem, o, {"rep": rep_peer(o)})

    for o in range(1, n_rep):
        rag(o, rep).start()

    for o in range(1, nz):
        agz(o, z_from(o)).wait_recv()

    def rep_rows(q):
        return pl.ds(pl.multiple_of(q * rblk, rblk), rblk)

    def agr(o, q):
        place = wsum_ref.at[rep_rows(q), own_cols]
        return remote(place, place, agr_sem, o, {"rep": rep_peer(o)})

    def agc(o, q, cols):
        place = wsum_ref.at[rep_rows(q), cols]
        return remote(place, place, agc_sem, o, {"shard": partner})

    for o in range(1, n_rep):
        agr(o, rep).start()
    agc(0, rep, own_cols).start()

    for o in range(1, nz):
        b3(o, z_from(o)).wait_recv()
    bias_all = bbuf3[0]
    for z in range(1, nz):
        bias_all = bias_all + bbuf3[z]
    bsum_ref[...] = bias_all

    for o in range(1, n_rep):
        agr(o, rep_from(o)).wait_recv()
        agc(o, rep_from(o), own_cols).start()
    for o in range(1, n_rep):
        rag(o, rep_from(o)).wait_recv()
    for o in range(n_rep):
        agc(o, rep_from(o), other_cols).wait_recv()

    p1.wait_send()
    b1.wait_send()
    for o in range(1, n_rep):
        p2(o).wait_send()
        b2(o, rep).wait_send()
        rrs(o).wait_send()
        rag(o, rep).wait_send()
        agr(o, rep).wait_send()
    for o in range(1, nz):
        p3(o).wait_send()
        b3(o, zi).wait_send()
        agz(o, zi).wait_send()
    for o in range(n_rep):
        agc(o, rep_from(o), own_cols).wait_send()

    @pl.loop(1, n_shard)
    def _(o):
        a2a(o).wait_send()


def step_call(n_rep, n_shard, feats, cot, weight, cbias, code, rows, touched, width):
    tok, d = feats.shape
    nz = n_shard // 2
    slots = code.shape[1]
    count = touched.shape[0]
    half = d // 2
    rblk = d // n_rep
    zblk = rblk // nz
    tblk = count // n_rep
    vmem = pl.BlockSpec(memory_space=pltpu.VMEM)

    def sems(n):
        return pltpu.SemaphoreType.DMA((2, n))

    return pl.pallas_call(
        functools.partial(step_kernel, n_rep, n_shard),
        out_shape=(
            jax.ShapeDtypeStruct((d, d), BF16),
            jax.ShapeDtypeStruct((d // 128, 128), F32),
            jax.ShapeDtypeStruct((tok, width), BF16),
            jax.ShapeDtypeStruct((count, width), BF16),
        ),
        in_specs=[vmem] * 7,
        out_specs=(vmem,) * 4,
        scratch_shapes=[
            pltpu.VMEM((tok, d), BF16),
            pltpu.VMEM((tok, d), BF16),
            pltpu.VMEM((d, half), F32),
            pltpu.VMEM((d, half), BF16),
            pltpu.VMEM((d, half), BF16),
            pltpu.VMEM((d, half), BF16),
            pltpu.VMEM((n_rep, rblk, half), BF16),
            pltpu.VMEM((nz, zblk, half), BF16),
            pltpu.VMEM((2, d // 128, 128), F32),
            pltpu.VMEM((n_rep, d // 128, 128), F32),
            pltpu.VMEM((nz, d // 128, 128), F32),
            pltpu.VMEM((n_shard, slots, width), BF16),
            pltpu.VMEM((n_shard, slots, width), BF16),
            pltpu.VMEM((count, width), F32),
            pltpu.VMEM((count, width), BF16),
            pltpu.VMEM((n_rep, tblk, width), BF16),
            sems(1),
            sems(n_rep),
            sems(nz),
            sems(1),
            sems(n_rep),
            sems(nz),
            sems(n_shard),
            sems(n_rep),
            sems(n_rep),
            sems(nz),
            sems(n_rep),
            sems(n_rep),
        ],
        compiler_params=pltpu.CompilerParams(
            collective_id=0, has_side_effects=True, vmem_limit_bytes=56 * 1024 * 1024
        ),
    )(feats, cot, weight, cbias, code, rows, touched)


def adagrad_rows(table_rows, accum_rows, grads):
    new_accum = accum_rows + jnp.mean(grads * grads, axis=1)
    new_rows = keep_rate * table_rows - learn_rate * grads / jnp.sqrt(new_accum)[:, None]
    return (new_rows, new_accum)


def per_device(
    n_rep,
    n_shard,
    features,
    cotangent,
    cross_weight,
    cross_bias,
    emb_table,
    row_accum,
    send_bags,
    slot_counts,
    recv_rows,
    touched_rows,
):
    tok, d = features.shape
    shard_rows, width = emb_table.shape
    feats = d // width - 1
    scale = 1.0 / jnp.sqrt(F32(tok * n_rep * n_shard))
    bags = send_bags[0]
    live = jnp.arange(bags.shape[1], dtype=jnp.int32)[None, :] < slot_counts[0][:, None]
    code = jnp.where(live, (bags // feats) * 8 + bags % feats, -8)
    touched = touched_rows[0]
    weight_sum, bias_sum, dense_grad, rows = step_call(
        n_rep,
        n_shard,
        features,
        cotangent,
        cross_weight,
        cross_bias[None, :],
        code,
        recv_rows[0],
        touched[:, None],
        width,
    )
    weight_grad = weight_sum.astype(F32) * scale
    bias_grad = bias_sum.reshape(-1) * scale
    row_range = jnp.arange(shard_rows, dtype=jnp.int32)
    hit = row_range[:, None] == touched[None, :]
    marks = jnp.any(hit, axis=1)
    row_grads = jnp.dot(hit.astype(BF16), rows, preferred_element_type=F32)
    upd_table, upd_accum = adagrad_rows(emb_table, row_accum, row_grads)
    new_table = jnp.where(marks[:, None], upd_table, emb_table)
    new_accum = jnp.where(marks, upd_accum, row_accum)
    return (weight_grad, bias_grad, dense_grad, new_table, new_accum)


def solution(mesh):
    in_specs = (
        P(("rep", "shard"), None),
        P(("rep", "shard"), None),
        P(),
        P(),
        P("shard", None),
        P("shard"),
        P(("rep", "shard"), None, None),
        P(("rep", "shard"), None),
        P(("rep", "shard"), None, None),
        P("shard", None),
    )
    out_specs = (P(), P(), P(("rep", "shard"), None), P("shard", None), P("shard"))
    return jax.shard_map(
        functools.partial(per_device, mesh.shape["rep"], mesh.shape["shard"]),
        mesh=mesh,
        in_specs=in_specs,
        out_specs=out_specs,
        check_vma=False,
    )
```

time: 303 us -> 76.6 us (0.25)
  waiting for transfers between devices: 161 us -> 0 us
  Pallas kernels: 0 us -> 55 us
  blocking collectives: 37.9 us -> 0 us
  matrix products: 41.2 us -> 4.32 us
  local copies, waits for them, and re-layouts: 25 us -> 5.83 us
  between operations: 14.2 us -> 0.68 us
  starting transfers between devices: 6.4 us -> 0 us
  other arithmetic: 16 us -> 10.3 us
    psum x2 -> x0, waiting for transfers between devices: 146 us -> none  [the longest x1 141 us: per_device(): weight_sum, bias_sum = lax.psum((weight_part, bias_part), ('rep', 'shard'))]
    pallas_call x0 -> x1, Pallas kernels: none -> 55 us  [step_call(): pl.pallas_call(functools.partial(step_kernel, n_rep, n_shard), out_shape=...]
    psum x1 -> x0, blocking collectives: 37.9 us -> none  [per_device(): weight_sum, bias_sum = lax.psum((weight_part, bias_part), ('rep', 'shard'))]
    dot_general x15 -> x1, matrix products: 41.2 us -> 4.32 us  [per_device(): row_grads = jnp.dot(hit.astype(BF16), rows, preferred_element_type=F32)]
    all_to_all x1 -> x0, waiting for transfers between devices: 15.4 us -> none  [per_device(): lax.all_to_all(outgoing, 'shard', split_axis=0, concat_axis=0, tiled=True)]
    gather x4 -> x0, local copies, waits for them, and re-layouts: 12.6 us -> none  [pick_bags(): flat_bags[positions][:, None] == bag_range[None, :]]
    all_to_all x1 -> x0, starting transfers between devices: 6.33 us -> none  [per_device(): lax.all_to_all(outgoing, 'shard', split_axis=0, concat_axis=0, tiled=True)]
    reduce_sum x2 -> x0, other arithmetic: 3.41 us -> none  [the longest x1 1.84 us: adagrad_rows(): new_accum = accum_rows + jnp.mean(grads * grads, axis=1)]
  transfers between devices with their start and end apart: 3 -> 0, of which waited for: 3 -> 0; matrix products, arithmetic and copies ran while one was open for 5% -> 0% of each run, Pallas kernels for 0% -> 0%
where the time goes in v1:
time: 76.6 us; the launch traced here: 76.2 us
  Pallas kernels  55 us (72%)
  other arithmetic  10.3 us (13%)
  local copies, waits for them, and re-layouts  5.83 us (8%)
  matrix products  4.32 us (6%)
    pallas_call x1, Pallas kernels, step_call(): pl.pallas_call(functools.partial(step_kernel, n_rep, n_shard), out_shape=...  55 us
    dot_general x1, matrix products, per_device(): row_grads = jnp.dot(hit.astype(BF16), rows, preferred_element_type=F32)  4.32 us
    unnamed x13, local copies, waits for them, and re-layouts  4.3 us
    mul x1, other arithmetic, per_device(): weight_grad = weight_sum.astype(F32) * scale  4.23 us
    select_n x1, other arithmetic, per_device(): new_table = jnp.where(marks[:, None], upd_table, emb_table)  2.64 us
    another operation x1, local copies, waits for them, and re-layouts, per_device(): touched[:, None]  1.54 us

profile of v1, /device:TPU:0, one launch (start us, length us, event | category | flops | bytes accessed | tf_op | source)
XLA Modules:
  0.0 76.2 jit_solution(12401000486717951975)
XLA Ops:
  0.6 1.5 %copy.22.touched_ref = s32[512,1]{1,0:T(8,128)} copy(s32[512,1]{0,1:T(1,128)} %bitcast.28) | data formatting | bytes 4096 | tf_op jit(solution)/shard_map/broadcast_in_dim;squeeze | solution.py:438
  2.2 1.4 %fusion.7.code_ref = s32[8,256]{1,0:T(8,128)} fusion(s32[1,8,256]{2,1,0:T(8,128)} %param.16, s32[8]{0:T(128)} %bitcast.31), kind=kLoop, calls=%fused_computation.14 | loop fusion | flops 32768 | bytes 16416 | tf_op jit(solution)/shard_map/jit(_where)/select_n | solution.py:427
  3.5 0.0 copy-start.4
  3.5 55.0 %shard_map.137 = (bf16[1024,1024]{1,0:T(8,128)(2,1)}, f32[8,128]{1,0:T(8,128)}, bf16[512,128]{1,0:T(8,128)(2,1)}, bf16[512,128]{1,0:T(8,128)(2,1)}) custom-call(bf16[512,1024]{1,0:T(8,128)(2,1)} %feat_ref.1, bf16[512,1024]{1,0:T(8,128)(2,1)} %cot_ref.1, bf16[1024,1024]{1,0:T(8,128)(2,1)} %w_ref.1, f32[1,1024]{1,0:T(1,128)} %bitcast.27, ...), custom_call_target="tpu_custom_call" | custom-call | tf_op jit(solution)/shard_map/pallas_call | solution.py:355
  58.6 0.0 copy-done.4
  58.6 0.0 copy-start.2
  58.6 0.0 copy-start
  58.6 4.3 %multiply_reduce_fusion = (f32[4096]{0:T(1024)S(1)}, f32[4096,128]{0,1:T(8,128)}) fusion(bf16[512,128]{1,0:T(8,128)(2,1)} %get-tuple-element.12, s32[512]{0:T(512)S(1)} %bitcast.29), kind=kOutput, calls=%fused_computation.6 | convolution fusion | flops 540012544 | bytes 2246656 | tf_op jit(solution)/shard_map/dot_general | solution.py:446
  62.9 0.9 %fusion.1 = pred[4096]{0:T(1024)(128)(4,1)S(1)} fusion(s32[512]{0:T(512)S(1)} %bitcast.30), kind=kLoop, calls=%fused_computation.2 | loop fusion | flops 4190208 | bytes 6144 | tf_op jit(solution)/shard_map/reduce_or | solution.py:445
  63.8 0.0 copy-done.2
  63.8 0.6 fusion.3
  64.4 0.0 copy-done
  64.4 1.8 %copy.23 = f32[4096,128]{0,1:T(8,128)} copy(f32[4096,128]{1,0:T(8,128)S(1)} %copy-done) | data formatting | bytes 4194304 | tf_op args[4]
  66.2 2.6 %subtract_select_fusion = f32[4096,128]{0,1:T(8,128)S(1)} fusion(f32[4096,128]{0,1:T(8,128)} %copy.23, f32[4096,128]{0,1:T(8,128)} %get-tuple-element.31, f32[4096]{0:T(1024)S(1)} %get-tuple-element.29, pred[4096]{0:T(1024)(128)(4,1)S(1)} %fusion.1), kind=kLoop, calls=%fused_computation.5 | loop fusion | flops 2621440 | bytes 6311936 | tf_op jit(solution)/shard_map/jit(_where)/select_n | solution.py:448
  68.9 1.8 %copy.25 = f32[4096,128]{1,0:T(8,128)} copy(f32[4096,128]{0,1:T(8,128)S(1)} %subtract_select_fusion) | data formatting | bytes 4194304
  70.7 0.0 copy-start.3
  70.7 0.0 copy-start.1
  70.7 4.2 %convert_multiply_fusion = f32[1024,1024]{1,0:T(8,128)} fusion(bf16[1024,1024]{1,0:T(8,128)(2,1)} %get-tuple-element.9), kind=kLoop, calls=%fused_computation.4 | loop fusion | flops 2097152 | bytes 6291456 | tf_op jit(solution)/shard_map/mul | solution.py:441
  74.9 0.0 copy-done.3
  74.9 0.6 multiply_bitcast_fusion
  75.5 0.0 copy-done.1
  75.5 0.7 copy.27
Async XLA Ops:
  3.5 55.0 %copy-start.4 = (s32[1,512]{1,0:T(1,128)S(1)}, s32[1,512]{1,0:T(1,128)}, u32[]{:S(2)}) copy-start(s32[1,512]{1,0:T(1,128)} %param.19) | copy-start | bytes 6148
  58.6 5.2 %copy-start.2 = (f32[4096]{0:T(1024)S(1)}, f32[4096]{0:T(1024)}, u32[]{:S(2)}) copy-start(f32[4096]{0:T(1024)} %param.15) | copy-start | bytes 49156
  58.6 5.9 %copy-start = (f32[4096,128]{1,0:T(8,128)S(1)}, f32[4096,128]{1,0:T(8,128)}, u32[]{:S(2)}) copy-start(f32[4096,128]{1,0:T(8,128)} %param.14) | copy-start | bytes 6291460
  70.7 4.2 %copy-start.3 = (f32[8,128]{1,0:T(8,128)S(1)}, f32[8,128]{1,0:T(8,128)}, u32[]{:S(2)}) copy-start(f32[8,128]{1,0:T(8,128)} %get-tuple-element.10) | copy-start | bytes 12292
  70.7 4.8 %copy-start.1 = (bf16[512,128]{1,0:T(8,128)(2,1)S(1)}, bf16[512,128]{1,0:T(8,128)(2,1)}, u32[]{:S(2)}) copy-start(bf16[512,128]{1,0:T(8,128)(2,1)} %get-tuple-element.39) | copy-start | bytes 393220

commit v2 on v1

v2 whole, which is shorter than its diff:
```python
import functools
import math

import jax
import jax.numpy as jnp
from jax import lax
from jax.experimental import pallas as pl
from jax.experimental.pallas import tpu as pltpu
from jax.sharding import PartitionSpec as P

learn_rate = 0.5
keep_rate = 0.9
MESH = pl.DeviceIdType.MESH
F32 = jnp.float32
BF16 = jnp.bfloat16


def step_kernel(
    n_rep,
    n_shard,
    feat_ref,
    cot_ref,
    w_ref,
    cbias_ref,
    bags_ref,
    counts_ref,
    rows_ref,
    touched_ref,
    wsum_ref,
    bsum_ref,
    dense_ref,
    rowt_ref,
    gated,
    ig,
    feat_t,
    wown,
    wsend,
    wpair,
    p1buf,
    p2buf,
    p3buf,
    bbuf1,
    bbuf2,
    bbuf3,
    outgoing,
    incoming,
    touched_col,
    rowacc,
    rowsend,
    rowbuf,
    p1_sem,
    p2_sem,
    p3_sem,
    b1_sem,
    b2_sem,
    b3_sem,
    a2a_sem,
    rrs_sem,
    rag_sem,
    agz_sem,
    agr_sem,
    agc_sem,
):
    nz = n_shard // 2
    rep = lax.axis_index("rep")
    shard = lax.axis_index("shard")
    core = lax.rem(shard, 2)
    zi = shard // 2
    partner = zi * 2 + (1 - core)
    tok, d = feat_ref.shape
    width = dense_ref.shape[1]
    feats = d // width - 1
    half = d // 2
    parts = half // 128
    rblk = d // n_rep
    zblk = rblk // nz
    touched_count = rowt_ref.shape[0]
    tblk = touched_count // n_rep
    slots = bags_ref.shape[1]
    inverse = (1 << 16) // feats + 1
    assert tok * feats * (inverse * feats - (1 << 16)) < 1 << 16

    def rep_peer(o):
        return lax.rem(rep + o, n_rep)

    def rep_from(o):
        return lax.rem(rep + n_rep - o, n_rep)

    def z_peer(o):
        return lax.rem(zi + o, nz)

    def z_from(o):
        return lax.rem(zi + nz - o, nz)

    def shard_peer(o):
        return lax.rem(shard + o, n_shard)

    def shard_from(o):
        return lax.rem(shard + n_shard - o, n_shard)

    def remote(src, dst, sems, index, target):
        return pltpu.make_async_remote_copy(
            src_ref=src,
            dst_ref=dst,
            send_sem=sems.at[0, index],
            recv_sem=sems.at[1, index],
            device_id=target,
            device_id_type=MESH,
        )

    def rep_rows(q):
        return pl.ds(pl.multiple_of(q * rblk, rblk), rblk)

    def z_rows(z):
        return pl.ds(pl.multiple_of(z * zblk, zblk), zblk)

    barrier = pltpu.get_barrier_semaphore()
    for o in range(1, n_shard):
        pl.semaphore_signal(
            barrier, inc=1, device_id={"shard": shard_peer(o)}, device_id_type=MESH
        )
    for o in range(1, n_rep):
        pl.semaphore_signal(barrier, inc=1, device_id={"rep": rep_peer(o)}, device_id_type=MESH)

    @pl.loop(0, tok // 128)
    def _(i):
        r = pl.ds(pl.multiple_of(i * 128, 128), 128)
        gated[r, :] = (cot_ref[r, :].astype(F32) * feat_ref[r, :].astype(F32)).astype(BF16)

    @pl.loop(0, d // 256)
    def _(i):
        r = pl.ds(pl.multiple_of(i * 256, 256), 256)
        feat_t[r, :] = jnp.transpose(feat_ref[:, r])

    def weight_pair(col_half, j, out, out_type):
        cols = pl.ds(pl.multiple_of(col_half * half + j * 256, 256), 256)

        @pl.loop(0, d // 256)
        def _(i):
            r = pl.ds(pl.multiple_of(i * 256, 256), 256)
            terms = jnp.dot(feat_t[r, :], gated[:, cols], preferred_element_type=F32)
            out[2 * j, r, :] = terms[:, :128].astype(out_type)
            out[2 * j + 1, r, :] = terms[:, 128:].astype(out_type)

    def p1(k):
        return remote(wsend.at[k], p1buf.at[k], p1_sem, k, {"shard": partner})

    for j in range(parts // 2):
        weight_pair(1 - core, j, wsend, BF16)
        if j == 0:
            pl.semaphore_wait(barrier, n_shard - 1 + n_rep - 1)
        p1(2 * j).start()
        p1(2 * j + 1).start()

    def p2(k, o):
        target = rep_peer(o)
        return remote(
            wpair.at[k, rep_rows(target), :],
            p2buf.at[k, o],
            p2_sem,
            k * n_rep + o,
            {"rep": target},
        )

    for j in range(parts // 2):
        weight_pair(core, j, wown, F32)
        for k in (2 * j, 2 * j + 1):
            p1(k).wait_recv()

            @pl.loop(0, n_rep)
            def _(i):
                r = rep_rows(i)
                wpair[k, r, :] = (wown[k, r, :] + p1buf[k, r, :].astype(F32)).astype(BF16)

            for o in range(1, n_rep):
                p2(k, o).start()

    bias_row = jnp.sum(gated[...].astype(F32), axis=0, keepdims=True)
    for j in range(d // 128):
        bbuf1[0, pl.ds(j, 1), :] = bias_row[:, j * 128 : (j + 1) * 128]
    b1 = remote(bbuf1.at[0], bbuf1.at[1], b1_sem, 0, {"shard": partner})
    b1.start()

    @pl.loop(0, d // 256)
    def _(i):
        c = pl.ds(pl.multiple_of(i * 256, 256), 256)
        linear = jnp.dot(feat_ref[...], w_ref[:, c], preferred_element_type=F32) + cbias_ref[:, c]
        back = lax.dot_general(
            gated[...], w_ref[c, :], (((1,), (1,)), ((), ())), preferred_element_type=F32
        )
        cot = cot_ref[:, c].astype(F32)
        ig[:, c] = (cot * linear + back + cot).astype(BF16)

    b1.wait_recv()
    bbuf2[rep] = bbuf1[0] + bbuf1[1]

    def b2(o, slot):
        return remote(bbuf2.at[slot], bbuf2.at[slot], b2_sem, o, {"rep": rep_peer(o)})

    for o in range(1, n_rep):
        b2(o, rep).start()

    def gather(dest):
        bags = bags_ref[pl.ds(dest, 1), :]
        place = lax.broadcasted_iota(jnp.int32, (1, slots), 1)
        sample = jnp.right_shift(bags * inverse, 16)
        code = jnp.where(place < counts_ref[0, dest], sample * 8 + (bags - sample * feats), -8)
        code = jnp.transpose(jnp.broadcast_to(code, (128, slots)))
        sample = jnp.right_shift(code, 3)
        feature = jnp.bitwise_and(code, 7)
        lane = lax.broadcasted_iota(jnp.int32, (slots, 128), 1)
        select = jnp.concatenate(
            [jnp.where(sample == lane + k * 128, 1.0, 0.0) for k in range(tok // 128)], axis=1
        ).astype(BF16)
        wide = jnp.dot(select, ig[:, width:], preferred_element_type=F32)
        picked = jnp.zeros((slots, width), F32)
        for f in range(feats):
            picked = jnp.where(feature == f, wide[:, f * width : (f + 1) * width], picked)
        return picked.astype(BF16)

    def a2a(o):
        dest = shard_peer(o)
        return remote(outgoing.at[dest], incoming.at[shard], a2a_sem, o, {"shard": dest})

    def a2a_in(o):
        src = shard_from(o)
        return remote(outgoing.at[src], incoming.at[src], a2a_sem, o, {"shard": src})

    @pl.loop(1, n_shard)
    def _(o):
        outgoing[shard_peer(o)] = gather(shard_peer(o))
        a2a(o).start()

    incoming[shard] = gather(shard)
    dense_ref[...] = ig[:, :width]
    touched_col[...] = jnp.transpose(
        jnp.broadcast_to(touched_ref[...], (128, touched_count))
    )

    def p3(k, o):
        target = z_peer(o)
        return remote(
            p2buf.at[k, 0, z_rows(target), :],
            p3buf.at[k, o],
            p3_sem,
            k * nz + o,
            {"shard": target * 2 + core},
        )

    def agz(k, o, z):
        place = wsum_ref.at[
            core * parts + k, pl.ds(pl.multiple_of(rep * rblk + z * zblk, zblk), zblk), :
        ]
        return remote(place, place, agz_sem, k * nz + o, {"shard": z_peer(o) * 2 + core})

    def agr(k, o, q):
        place = wsum_ref.at[core * parts + k, rep_rows(q), :]
        return remote(place, place, agr_sem, k * n_rep + o, {"rep": rep_peer(o)})

    def agc(k, o, q, side):
        place = wsum_ref.at[side * parts + k, rep_rows(q), :]
        return remote(place, place, agc_sem, k * n_rep + o, {"shard": partner})

    for t in range(parts + 2):
        if t < parts:
            k = t
            for o in range(1, n_rep):
                p2(k, o).wait_recv()
            total = wpair[k, rep_rows(rep), :].astype(F32)
            for o in range(1, n_rep):
                total = total + p2buf[k, o].astype(F32)
            p2buf[k, 0] = total.astype(BF16)
            for o in range(1, nz):
                p3(k, o).start()
        if 1 <= t <= parts:
            k = t - 1
            for o in range(1, nz):
                p3(k, o).wait_recv()
            block = p2buf[k, 0, z_rows(zi), :].astype(F32)
            for o in range(1, nz):
                block = block + p3buf[k, o].astype(F32)
            mine = pl.ds(pl.multiple_of(rep * rblk + zi * zblk, zblk), zblk)
            wsum_ref[core * parts + k, mine, :] = block.astype(BF16)
            for o in range(1, nz):
                agz(k, o, zi).start()
        if 2 <= t:
            k = t - 2
            for o in range(1, nz):
                agz(k, o, z_from(o)).wait_recv()
            for o in range(1, n_rep):
                agr(k, o, rep).start()
            agc(k, 0, rep, core).start()

    for o in range(1, n_rep):
        b2(o, rep_from(o)).wait_recv()
    bias_rep = bbuf2[0]
    for q in range(1, n_rep):
        bias_rep = bias_rep + bbuf2[q]
    bbuf3[zi] = bias_rep

    def b3(o, slot):
        return remote(
            bbuf3.at[slot], bbuf3.at[slot], b3_sem, o, {"shard": z_peer(o) * 2 + core}
        )

    for o in range(1, nz):
        b3(o, zi).start()

    def add_source(src):
        rows = rows_ref[pl.ds(src, 1), :]
        select = jnp.concatenate(
            [
                jnp.where(touched_col[...] == rows[:, k * 128 : (k + 1) * 128], 1.0, 0.0)
                for k in range(slots // 128)
            ],
            axis=1,
        ).astype(BF16)
        return jnp.dot(select, incoming[src], preferred_element_type=F32)

    rowacc[...] = add_source(shard)

    @pl.loop(1, n_shard)
    def _(o):
        a2a_in(o).wait_recv()
        rowacc[...] += add_source(shard_from(o))

    rowsend[...] = rowacc[...].astype(BF16)

    def rrs(o):
        target = rep_peer(o)
        r = pl.ds(pl.multiple_of(target * tblk, tblk), tblk)
        return remote(rowsend.at[r, :], rowbuf.at[o], rrs_sem, o, {"rep": target})

    for o in range(1, n_rep):
        rrs(o).start()

    for k in range(parts // 2):
        for o in range(1, n_rep):
            agr(k, o, rep_from(o)).wait_recv()
            agc(k, o, rep_from(o), core).start()

    for o in range(1, n_rep):
        rrs(o).wait_recv()
    own = pl.ds(pl.multiple_of(rep * tblk, tblk), tblk)
    row_total = rowacc[own, :]
    for o in range(1, n_rep):
        row_total = row_total + rowbuf[o].astype(F32)
    rowt_ref[own, :] = row_total.astype(BF16)

    def rag(o, q):
        place = rowt_ref.at[pl.ds(pl.multiple_of(q * tblk, tblk), tblk), :]
        return remote(place, place, rag_sem, o, {"rep": rep_peer(o)})

    for o in range(1, n_rep):
        rag(o, rep).start()

    for o in range(1, nz):
        b3(o, z_from(o)).wait_recv()
    bias_all = bbuf3[0]
    for z in range(1, nz):
        bias_all = bias_all + bbuf3[z]
    bsum_ref[...] = bias_all

    for k in range(parts // 2, parts):
        for o in range(1, n_rep):
            agr(k, o, rep_from(o)).wait_recv()
            agc(k, o, rep_from(o), core).start()
    for o in range(1, n_rep):
        rag(o, rep_from(o)).wait_recv()
    for k in range(parts):
        for o in range(n_rep):
            agc(k, o, rep_from(o), 1 - core).wait_recv()

    b1.wait_send()
    for o in range(1, n_rep):
        b2(o, rep).wait_send()
        rrs(o).wait_send()
        rag(o, rep).wait_send()
    for o in range(1, nz):
        b3(o, zi).wait_send()
    for k in range(parts):
        p1(k).wait_send()
        for o in range(1, n_rep):
            p2(k, o).wait_send()
            agr(k, o, rep).wait_send()
        for o in range(1, nz):
            p3(k, o).wait_send()
            agz(k, o, zi).wait_send()
        for o in range(n_rep):
            agc(k, o, rep_from(o), core).wait_send()

    @pl.loop(1, n_shard)
    def _(o):
        a2a(o).wait_send()


def step_call(n_rep, n_shard, feats, cot, weight, cbias, bags, counts, rows, touched, width):
    tok, d = feats.shape
    nz = n_shard // 2
    slots = bags.shape[1]
    count = touched.shape[1]
    half = d // 2
    parts = half // 128
    rblk = d // n_rep
    zblk = rblk // nz
    tblk = count // n_rep
    vmem = pl.BlockSpec(memory_space=pltpu.VMEM)
    smem = pl.BlockSpec(memory_space=pltpu.SMEM)

    def sems(n):
        return pltpu.SemaphoreType.DMA((2, n))

    return pl.pallas_call(
        functools.partial(step_kernel, n_rep, n_shard),
        out_shape=(
            jax.ShapeDtypeStruct((2 * parts, d, 128), BF16),
            jax.ShapeDtypeStruct((d // 128, 128), F32),
            jax.ShapeDtypeStruct((tok, width), BF16),
            jax.ShapeDtypeStruct((count, width), BF16),
        ),
        in_specs=[vmem] * 5 + [smem] + [vmem] * 2,
        out_specs=(vmem,) * 4,
        scratch_shapes=[
            pltpu.VMEM((tok, d), BF16),
            pltpu.VMEM((tok, d), BF16),
            pltpu.VMEM((d, tok), BF16),
            pltpu.VMEM((parts, d, 128), F32),
            pltpu.VMEM((parts, d, 128), BF16),
            pltpu.VMEM((parts, d, 128), BF16),
            pltpu.VMEM((parts, d, 128), BF16),
            pltpu.VMEM((parts, n_rep, rblk, 128), BF16),
            pltpu.VMEM((parts, nz, zblk, 128), BF16),
            pltpu.VMEM((2, d // 128, 128), F32),
            pltpu.VMEM((n_rep, d // 128, 128), F32),
            pltpu.VMEM((nz, d // 128, 128), F32),
            pltpu.VMEM((n_shard, slots, width), BF16),
            pltpu.VMEM((n_shard, slots, width), BF16),
            pltpu.VMEM((count, 128), jnp.int32),
            pltpu.VMEM((count, width), F32),
            pltpu.VMEM((count, width), BF16),
            pltpu.VMEM((n_rep, tblk, width), BF16),
            sems(parts),
            sems(parts * n_rep),
            sems(parts * nz),
            sems(1),
            sems(n_rep),
            sems(nz),
            sems(n_shard),
            sems(n_rep),
            sems(n_rep),
            sems(parts * nz),
            sems(parts * n_rep),
            sems(parts * n_rep),
        ],
        compiler_params=pltpu.CompilerParams(
            collective_id=0, has_side_effects=True, vmem_limit_bytes=56 * 1024 * 1024
        ),
    )(feats, cot, weight, cbias, bags, counts, rows, touched)


def update_kernel(
    scale,
    wsum_ref,
    bsum_ref,
    dense_ref,
    rowt_ref,
    touched_ref,
    accum_ref,
    table_ref,
    wgrad_ref,
    bgrad_ref,
    dense_out_ref,
    accum_out_ref,
    table_out_ref,
):
    step = pl.program_id(0)
    count, width = rowt_ref.shape
    for c in range(wsum_ref.shape[0]):
        wgrad_ref[:, c * 128 : (c + 1) * 128] = wsum_ref[c].astype(F32) * scale
    dense_out_ref[...] = dense_ref[...]
    bgrad_ref[...] = bsum_ref[...] * scale

    source = jnp.concatenate([rowt_ref[...], jnp.ones((count, 128), BF16)], axis=1)
    blocks = table_ref.shape[0] // 128
    for i in range(blocks):
        block = step * blocks + i
        row_ids = block * 128 + lax.broadcasted_iota(jnp.int32, (128, count), 0)
        select = jnp.where(row_ids == touched_ref[...], 1.0, 0.0).astype(BF16)
        spread = jnp.dot(select, source, preferred_element_type=F32)
        grads = spread[:, :width]
        flipped = jnp.transpose(grads)
        square = jnp.sum(flipped * flipped, axis=0, keepdims=True)
        new_accum = accum_ref[pl.ds(block, 1), :] + square / width
        accum_out_ref[pl.ds(block, 1), :] = new_accum
        rate = jnp.transpose(jnp.broadcast_to(learn_rate / jnp.sqrt(new_accum), (width, 128)))
        r = pl.ds(i * 128, 128)
        rows = table_ref[r, :]
        table_out_ref[r, :] = jnp.where(
            spread[:, width:] > 0.5, keep_rate * rows - grads * rate, rows
        )


def update_call(scale, wsum, bsum, dense, rowt, touched, accum, table):
    pieces, d, _ = wsum.shape
    tok, width = dense.shape
    count = rowt.shape[0]
    shard_rows = table.shape[0]
    steps = 8

    def whole(shape):
        return pl.BlockSpec(shape, lambda i: (0,) * len(shape))

    return pl.pallas_call(
        functools.partial(update_kernel, scale),
        grid=(steps,),
        in_specs=[
            pl.BlockSpec((pieces, d // steps, 128), lambda i: (0, i, 0)),
            whole(bsum.shape),
            pl.BlockSpec((tok // steps, width), lambda i: (i, 0)),
            whole((count, width)),
            whole((1, count)),
            whole(accum.shape),
            pl.BlockSpec((shard_rows // steps, width), lambda i: (i, 0)),
        ],
        out_specs=(
            pl.BlockSpec((d // steps, d), lambda i: (i, 0)),
            whole(bsum.shape),
            pl.BlockSpec((tok // steps, width), lambda i: (i, 0)),
            whole(accum.shape),
            pl.BlockSpec((shard_rows // steps, width), lambda i: (i, 0)),
        ),
        out_shape=(
            jax.ShapeDtypeStruct((d, d), F32),
            jax.ShapeDtypeStruct(bsum.shape, F32),
            jax.ShapeDtypeStruct((tok, width), BF16),
            jax.ShapeDtypeStruct(accum.shape, F32),
            jax.ShapeDtypeStruct(table.shape, F32),
        ),
        compiler_params=pltpu.CompilerParams(vmem_limit_bytes=40 * 1024 * 1024),
    )(wsum, bsum, dense, rowt, touched, accum, table)


def per_device(
    n_rep,
    n_shard,
    features,
    cotangent,
    cross_weight,
    cross_bias,
    emb_table,
    row_accum,
    send_bags,
    slot_counts,
    recv_rows,
    touched_rows,
):
    tok = features.shape[0]
    width = emb_table.shape[1]
    scale = 1.0 / math.sqrt(tok * n_rep * n_shard)
    weight_sum, bias_sum, dense, rows = step_call(
        n_rep,
        n_shard,
        features,
        cotangent,
        cross_weight,
        cross_bias[None, :],
        send_bags[0],
        slot_counts,
        recv_rows[0],
        touched_rows,
        width,
    )
    weight_grad, bias_grad, dense_grad, new_accum, new_table = update_call(
        scale, weight_sum, bias_sum, dense, rows, touched_rows, row_accum.reshape(-1, 128), emb_table
    )
    return (weight_grad, bias_grad.reshape(-1), dense_grad, new_table, new_accum.reshape(-1))


def solution(mesh):
    in_specs = (
        P(("rep", "shard"), None),
        P(("rep", "shard"), None),
        P(),
        P(),
        P("shard", None),
        P("shard"),
        P(("rep", "shard"), None, None),
        P(("rep", "shard"), None),
        P(("rep", "shard"), None, None),
        P("shard", None),
    )
    out_specs = (P(), P(), P(("rep", "shard"), None), P("shard", None), P("shard"))
    return jax.shard_map(
        functools.partial(per_device, mesh.shape["rep"], mesh.shape["shard"]),
        mesh=mesh,
        in_specs=in_specs,
        out_specs=out_specs,
        check_vma=False,
    )
```

time: 76.6 us -> 68 us (0.89)
  other arithmetic: 10.3 us -> 0 us
  Pallas kernels: 55 us -> 63 us
  matrix products: 4.32 us -> 0 us
  local copies, waits for them, and re-layouts: 5.83 us -> 4.08 us
    pallas_call x0 -> x1, Pallas kernels: none -> 6.26 us  [update_call(): pl.pallas_call(functools.partial(update_kernel, scale), grid=(steps,), in...]
    mul x2 -> x0, other arithmetic: 4.83 us -> none  [the longest x1 4.23 us: per_device(): weight_grad = weight_sum.astype(F32) * scale]
    select_n x3 -> x0, other arithmetic: 4.61 us -> none  [the longest x1 2.64 us: per_device(): new_table = jnp.where(marks[:, None], upd_table, emb_table)]
    dot_general x1 -> x0, matrix products: 4.32 us -> none  [per_device(): row_grads = jnp.dot(hit.astype(BF16), rows, preferred_element_type=F32)]
    pallas_call x1, Pallas kernels: 55 us -> 56.7 us  [step_call(): pl.pallas_call(functools.partial(step_kernel, n_rep, n_shard), out_shape=...]
    another operation x1 -> x0, local copies, waits for them, and re-layouts: 1.54 us -> none  [per_device(): touched[:, None]]
    reduce_or x1 -> x0, other arithmetic: 0.89 us -> none  [per_device(): marks = jnp.any(hit, axis=1)]
    unnamed x13 -> x14, local copies, waits for them, and re-layouts: 4.3 us -> 4.08 us
where the time goes in v2:
time: 68 us; the launch traced here: 67.8 us
  Pallas kernels  63 us (93%)
  local copies, waits for them, and re-layouts  4.08 us (6%)
  between operations  0.7 us (1%)
    pallas_call x1, Pallas kernels, step_call(): pl.pallas_call(functools.partial(step_kernel, n_rep, n_shard), out_shape=...  56.7 us
    pallas_call x1, Pallas kernels, update_call(): pl.pallas_call(functools.partial(update_kernel, scale), grid=(steps,), in...  6.26 us
    unnamed x14, local copies, waits for them, and re-layouts  4.08 us

profile of v2, /device:TPU:0, one launch (start us, length us, event | category | flops | bytes accessed | tf_op | source)
XLA Modules:
  0.0 67.8 jit_solution(5717001681005027884)
XLA Ops:
  0.6 0.0 copy-start
  0.6 0.0 copy-start.4
  0.7 0.0 copy-start.5
  0.7 56.7 %shard_map.137 = (bf16[8,1024,128]{2,1,0:T(8,128)(2,1)}, f32[8,128]{1,0:T(8,128)}, bf16[512,128]{1,0:T(8,128)(2,1)}, bf16[512,128]{1,0:T(8,128)(2,1)}) custom-call(bf16[512,1024]{1,0:T(8,128)(2,1)} %feat_ref.1, bf16[512,1024]{1,0:T(8,128)(2,1)} %cot_ref.1, bf16[1024,1024]{1,0:T(8,128)(2,1)} %w_ref.1, f32[1,1024]{1,0:T(1,128)} %bitcast.9, s32[8,256]{1,0:T(8,128)} %bitcast.7, ...), custom_call_target="tpu_custom_call" | custom-call | tf_op jit(solution)/shard_map/pallas_call | solution.py:413
  57.4 0.0 copy-done
  57.4 0.0 copy-done.4
  57.4 0.0 copy-done.5
  57.4 0.0 copy-start.1
  57.4 1.6 %copy-done.1 = bf16[8,1024,128]{2,1,0:T(8,128)(2,1)S(1)} copy-done((bf16[8,1024,128]{2,1,0:T(8,128)(2,1)S(1)}, bf16[8,1024,128]{2,1,0:T(8,128)(2,1)}, u32[]{:S(2)}) %copy-start.1) | copy-done | bytes 2097176
  59.0 0.0 copy-start.2
  59.0 0.9 %copy-done.2 = bf16[512,128]{1,0:T(8,128)(2,1)S(1)} copy-done((bf16[512,128]{1,0:T(8,128)(2,1)S(1)}, bf16[512,128]{1,0:T(8,128)(2,1)}, u32[]{:S(2)}) %copy-start.2) | copy-done | bytes 131096
  59.9 0.0 copy-start.3
  59.9 0.9 %copy-done.3 = bf16[512,128]{1,0:T(8,128)(2,1)S(1)} copy-done((bf16[512,128]{1,0:T(8,128)(2,1)S(1)}, bf16[512,128]{1,0:T(8,128)(2,1)}, u32[]{:S(2)}) %copy-start.3) | copy-done | bytes 131096
  60.8 0.0 copy-start.6
  60.8 0.7 %copy-done.6 = f32[8,128]{1,0:T(8,128)S(1)} copy-done((f32[8,128]{1,0:T(8,128)S(1)}, f32[8,128]{1,0:T(8,128)}, u32[]{:S(2)}) %copy-start.6) | copy-done | bytes 4120
  61.5 6.3 %shard_map.138 = (f32[1024,1024]{1,0:T(8,128)}, f32[8,128]{1,0:T(8,128)}, bf16[512,128]{1,0:T(8,128)(2,1)}, f32[32,128]{1,0:T(8,128)}, f32[4096,128]{1,0:T(8,128)}) custom-call(bf16[8,1024,128]{2,1,0:T(8,128)(2,1)S(1)} %copy-done.1, f32[8,128]{1,0:T(8,128)S(1)} %copy-done.6, bf16[512,128]{1,0:T(8,128)(2,1)S(1)} %copy-done.2, bf16[512,128]{1,0:T(8,128)(2,1)S(1)} %copy-done.3, ...), custom_call_target="tpu_custom_call" | custom-call | tf_op jit(solution)/shard_map/pallas_call | solution.py:513
Async XLA Ops:
  0.6 56.8 %copy-start = (f32[4096,128]{1,0:T(8,128)S(1)}, f32[4096,128]{1,0:T(8,128)}, u32[]{:S(2)}) copy-start(f32[4096,128]{1,0:T(8,128)} %table_ref.1) | copy-start | bytes 6291460
  0.6 56.8 %copy-start.4 = (f32[4096]{0:T(1024)S(1)}, f32[4096]{0:T(1024)}, u32[]{:S(2)}) copy-start(f32[4096]{0:T(1024)} %param.15) | copy-start | bytes 49156
  0.7 56.8 %copy-start.5 = (s32[1,512]{1,0:T(1,128)S(1)}, s32[1,512]{1,0:T(1,128)}, u32[]{:S(2)}) copy-start(s32[1,512]{1,0:T(1,128)} %touched_ref.3) | copy-start | bytes 6148
  57.4 1.6 %copy-start.1 = (bf16[8,1024,128]{2,1,0:T(8,128)(2,1)S(1)}, bf16[8,1024,128]{2,1,0:T(8,128)(2,1)}, u32[]{:S(2)}) copy-start(bf16[8,1024,128]{2,1,0:T(8,128)(2,1)} %get-tuple-element.14.wsum_ref) | copy-start | bytes 6291460
  59.0 0.9 %copy-start.2 = (bf16[512,128]{1,0:T(8,128)(2,1)S(1)}, bf16[512,128]{1,0:T(8,128)(2,1)}, u32[]{:S(2)}) copy-start(bf16[512,128]{1,0:T(8,128)(2,1)} %get-tuple-element.16.dense_ref) | copy-start | bytes 393220
  59.9 0.9 %copy-start.3 = (bf16[512,128]{1,0:T(8,128)(2,1)S(1)}, bf16[512,128]{1,0:T(8,128)(2,1)}, u32[]{:S(2)}) copy-start(bf16[512,128]{1,0:T(8,128)(2,1)} %get-tuple-element.17.rowt_ref) | copy-start | bytes 393220
  60.8 0.7 %copy-start.6 = (f32[8,128]{1,0:T(8,128)S(1)}, f32[8,128]{1,0:T(8,128)}, u32[]{:S(2)}) copy-start(f32[8,128]{1,0:T(8,128)} %get-tuple-element.15.bsum_ref) | copy-start | bytes 12292

commit v3 on v2

--- a/solution.py
+++ b/solution.py
@@ -20,16 +20,18 @@
     n_shard,
     feat_ref,
     cot_ref,
-    w_ref,
+    w_hbm,
     cbias_ref,
     bags_ref,
     counts_ref,
     rows_ref,
     touched_ref,
-    wsum_ref,
+    wsum_hbm,
     bsum_ref,
     dense_ref,
     rowt_ref,
+    w_ref,
+    wsum_ref,
     gated,
     ig,
     feat_t,
@@ -60,6 +62,8 @@
     agz_sem,
     agr_sem,
     agc_sem,
+    w_sem,
+    out_sem,
 ):
     nz = n_shard // 2
     rep = lax.axis_index("rep")
@@ -114,6 +118,8 @@
     def z_rows(z):
         return pl.ds(pl.multiple_of(z * zblk, zblk), zblk)
 
+    w_copy = pltpu.make_async_copy(w_hbm, w_ref, w_sem.at[0])
+    w_copy.start()
     barrier = pltpu.get_barrier_semaphore()
     for o in range(1, n_shard):
         pl.semaphore_signal(
@@ -180,6 +186,8 @@
         bbuf1[0, pl.ds(j, 1), :] = bias_row[:, j * 128 : (j + 1) * 128]
     b1 = remote(bbuf1.at[0], bbuf1.at[1], b1_sem, 0, {"shard": partner})
     b1.start()
+
+    w_copy.wait()
 
     @pl.loop(0, d // 256)
     def _(i):
@@ -226,16 +234,11 @@
         src = shard_from(o)
         return remote(outgoing.at[src], incoming.at[src], a2a_sem, o, {"shard": src})
 
-    @pl.loop(1, n_shard)
-    def _(o):
-        outgoing[shard_peer(o)] = gather(shard_peer(o))
-        a2a(o).start()
-
-    incoming[shard] = gather(shard)
-    dense_ref[...] = ig[:, :width]
-    touched_col[...] = jnp.transpose(
-        jnp.broadcast_to(touched_ref[...], (128, touched_count))
-    )
+    def send_slots(low, high):
+        @pl.loop(low, high)
+        def _(o):
+            outgoing[shard_peer(o)] = gather(shard_peer(o))
+            a2a(o).start()
 
     def p3(k, o):
         target = z_peer(o)
@@ -261,6 +264,7 @@
         place = wsum_ref.at[side * parts + k, rep_rows(q), :]
         return remote(place, place, agc_sem, k * n_rep + o, {"shard": partner})
 
+    cuts = (1, n_shard // 2 - 1, n_shard - 2, n_shard)
     for t in range(parts + 2):
         if t < parts:
             k = t
@@ -272,6 +276,8 @@
             p2buf[k, 0] = total.astype(BF16)
             for o in range(1, nz):
                 p3(k, o).start()
+            if t < 3:
+                send_slots(cuts[t], cuts[t + 1])
         if 1 <= t <= parts:
             k = t - 1
             for o in range(1, nz):
@@ -291,6 +297,11 @@
                 agr(k, o, rep).start()
             agc(k, 0, rep, core).start()
 
+    incoming[shard] = gather(shard)
+    dense_ref[...] = ig[:, :width]
+    touched_col[...] = jnp.transpose(
+        jnp.broadcast_to(touched_ref[...], (128, touched_count))
+    )
     for o in range(1, n_rep):
         b2(o, rep_from(o)).wait_recv()
     bias_rep = bbuf2[0]
@@ -334,10 +345,15 @@
     for o in range(1, n_rep):
         rrs(o).start()
 
+    def write_out(side, k):
+        piece = side * parts + k
+        return pltpu.make_async_copy(wsum_ref.at[piece], wsum_hbm.at[piece], out_sem.at[piece])
+
     for k in range(parts // 2):
         for o in range(1, n_rep):
             agr(k, o, rep_from(o)).wait_recv()
             agc(k, o, rep_from(o), core).start()
+        write_out(core, k).start()
 
     for o in range(1, n_rep):
         rrs(o).wait_recv()
@@ -365,11 +381,13 @@
         for o in range(1, n_rep):
             agr(k, o, rep_from(o)).wait_recv()
             agc(k, o, rep_from(o), core).start()
+        write_out(core, k).start()
     for o in range(1, n_rep):
         rag(o, rep_from(o)).wait_recv()
     for k in range(parts):
         for o in range(n_rep):
             agc(k, o, rep_from(o), 1 - core).wait_recv()
+        write_out(1 - core, k).start()
 
     b1.wait_send()
     for o in range(1, n_rep):
@@ -388,6 +406,8 @@
             agz(k, o, zi).wait_send()
         for o in range(n_rep):
             agc(k, o, rep_from(o), core).wait_send()
+        write_out(core, k).wait()
+        write_out(1 - core, k).wait()
 
     @pl.loop(1, n_shard)
     def _(o):
@@ -406,6 +426,7 @@
     tblk = count // n_rep
     vmem = pl.BlockSpec(memory_space=pltpu.VMEM)
     smem = pl.BlockSpec(memory_space=pltpu.SMEM)
+    hbm = pl.BlockSpec(memory_space=pl.ANY)
 
     def sems(n):
         return pltpu.SemaphoreType.DMA((2, n))
@@ -418,9 +439,11 @@
             jax.ShapeDtypeStruct((tok, width), BF16),
             jax.ShapeDtypeStruct((count, width), BF16),
         ),
-        in_specs=[vmem] * 5 + [smem] + [vmem] * 2,
-        out_specs=(vmem,) * 4,
+        in_specs=[vmem, vmem, hbm, vmem, vmem, smem, vmem, vmem],
+        out_specs=(hbm, vmem, vmem, vmem),
         scratch_shapes=[
+            pltpu.VMEM((d, d), BF16),
+            pltpu.VMEM((2 * parts, d, 128), BF16),
             pltpu.VMEM((tok, d), BF16),
             pltpu.VMEM((tok, d), BF16),
             pltpu.VMEM((d, tok), BF16),
@@ -451,9 +474,11 @@
             sems(parts * nz),
             sems(parts * n_rep),
             sems(parts * n_rep),
+            pltpu.SemaphoreType.DMA((1,)),
+            pltpu.SemaphoreType.DMA((2 * parts,)),
         ],
         compiler_params=pltpu.CompilerParams(
-            collective_id=0, has_side_effects=True, vmem_limit_bytes=56 * 1024 * 1024
+            collective_id=0, has_side_effects=True, vmem_limit_bytes=60 * 1024 * 1024
         ),
     )(feats, cot, weight, cbias, bags, counts, rows, touched)
 
@@ -536,7 +561,7 @@
             jax.ShapeDtypeStruct(accum.shape, F32),
             jax.ShapeDtypeStruct(table.shape, F32),
         ),
-        compiler_params=pltpu.CompilerParams(vmem_limit_bytes=40 * 1024 * 1024),
+        compiler_params=pltpu.CompilerParams(vmem_limit_bytes=60 * 1024 * 1024),
     )(wsum, bsum, dense, rowt, touched, accum, table)
 
 

time: 68 us -> 65.1 us (0.957)
  local copies, waits for them, and re-layouts: 4.08 us -> 0 us
  Pallas kernels: 63 us -> 64.1 us
    unnamed x14 -> x0, local copies, waits for them, and re-layouts: 4.08 us -> none
    pallas_call x1, Pallas kernels: 6.26 us -> 8.73 us  [update_call(): pl.pallas_call(functools.partial(update_kernel, scale), grid=(steps,), in...]
    pallas_call x1, Pallas kernels: 56.7 us -> 55.4 us  [step_call(): pl.pallas_call(functools.partial(step_kernel, n_rep, n_shard), out_shape=...]
where the time goes in v3:
time: 65.1 us; the launch traced here: 64.7 us
  Pallas kernels  64.1 us (98%)
    pallas_call x1, Pallas kernels, step_call(): pl.pallas_call(functools.partial(step_kernel, n_rep, n_shard), out_shape=...  55.4 us
    pallas_call x1, Pallas kernels, update_call(): pl.pallas_call(functools.partial(update_kernel, scale), grid=(steps,), in...  8.73 us

profile of v3, /device:TPU:0, one launch (start us, length us, event | category | flops | bytes accessed | tf_op | source)
XLA Modules:
  0.0 64.7 jit_solution(3723922642757635259)
XLA Ops:
  0.6 55.4 %shard_map.137 = (bf16[8,1024,128]{2,1,0:T(8,128)(2,1)}, f32[8,128]{1,0:T(8,128)}, bf16[512,128]{1,0:T(8,128)(2,1)}, bf16[512,128]{1,0:T(8,128)(2,1)}) custom-call(bf16[512,1024]{1,0:T(8,128)(2,1)} %feat_ref.1, bf16[512,1024]{1,0:T(8,128)(2,1)} %cot_ref.1, bf16[1024,1024]{1,0:T(8,128)(2,1)} %w_hbm.1, f32[1,1024]{1,0:T(1,128)} %bitcast.9, s32[8,256]{1,0:T(8,128)} %bitcast.7, ...), custom_call_target="tpu_custom_call" | custom-call | tf_op jit(solution)/shard_map/pallas_call | solution.py:434
  56.0 8.7 %shard_map.138 = (f32[1024,1024]{1,0:T(8,128)}, f32[8,128]{1,0:T(8,128)}, bf16[512,128]{1,0:T(8,128)(2,1)}, f32[32,128]{1,0:T(8,128)}, f32[4096,128]{1,0:T(8,128)}) custom-call(bf16[8,1024,128]{2,1,0:T(8,128)(2,1)} %get-tuple-element.14.wsum_ref, f32[8,128]{1,0:T(8,128)} %get-tuple-element.15.bsum_ref, bf16[512,128]{1,0:T(8,128)(2,1)} %get-tuple-element.16.dense_ref, ...), custom_call_target="tpu_custom_call" | custom-call | tf_op jit(solution)/shard_map/pallas_call | solution.py:538

commit v4 on v3

--- a/solution.py
+++ b/solution.py
@@ -506,23 +506,24 @@
     bgrad_ref[...] = bsum_ref[...] * scale
 
     source = jnp.concatenate([rowt_ref[...], jnp.ones((count, 128), BF16)], axis=1)
-    blocks = table_ref.shape[0] // 128
+    rows_here = table_ref.shape[0]
+    blocks = rows_here // 128
+    row_ids = step * rows_here + lax.broadcasted_iota(jnp.int32, (rows_here, count), 0)
+    select = jnp.where(row_ids == touched_ref[...], 1.0, 0.0).astype(BF16)
+    spread = jnp.dot(select, source, preferred_element_type=F32)
+    grads = spread[:, :width]
+    flipped = jnp.transpose(grads)
+    square = jnp.sum(flipped * flipped, axis=0, keepdims=True) / width
+    rates = []
     for i in range(blocks):
-        block = step * blocks + i
-        row_ids = block * 128 + lax.broadcasted_iota(jnp.int32, (128, count), 0)
-        select = jnp.where(row_ids == touched_ref[...], 1.0, 0.0).astype(BF16)
-        spread = jnp.dot(select, source, preferred_element_type=F32)
-        grads = spread[:, :width]
-        flipped = jnp.transpose(grads)
-        square = jnp.sum(flipped * flipped, axis=0, keepdims=True)
-        new_accum = accum_ref[pl.ds(block, 1), :] + square / width
-        accum_out_ref[pl.ds(block, 1), :] = new_accum
-        rate = jnp.transpose(jnp.broadcast_to(learn_rate / jnp.sqrt(new_accum), (width, 128)))
-        r = pl.ds(i * 128, 128)
-        rows = table_ref[r, :]
-        table_out_ref[r, :] = jnp.where(
-            spread[:, width:] > 0.5, keep_rate * rows - grads * rate, rows
-        )
+        place = pl.ds(step * blocks + i, 1)
+        new_accum = accum_ref[place, :] + square[:, i * 128 : (i + 1) * 128]
+        accum_out_ref[place, :] = new_accum
+        rates.append(learn_rate / jnp.sqrt(new_accum))
+    rate = jnp.concatenate(rates, axis=1)
+    rate = jnp.transpose(jnp.broadcast_to(rate, (width, rows_here)))
+    rows = table_ref[...]
+    table_out_ref[...] = jnp.where(spread[:, width:] > 0.5, keep_rate * rows - grads * rate, rows)
 
 
 def update_call(scale, wsum, bsum, dense, rowt, touched, accum, table):

time: 65.1 us -> 65 us (level)
  no operation moved by 1% of the time
where the time goes in v4:
time: 65 us; the launch traced here: 64.7 us
  Pallas kernels  64.1 us (99%)
    pallas_call x1, Pallas kernels, step_call(): pl.pallas_call(functools.partial(step_kernel, n_rep, n_shard), out_shape=...  55.4 us
    pallas_call x1, Pallas kernels, update_call(): pl.pallas_call(functools.partial(update_kernel, scale), grid=(steps,), in...  8.68 us

profile of v4, /device:TPU:0, one launch (start us, length us, event | category | flops | bytes accessed | tf_op | source)
XLA Modules:
  0.0 64.7 jit_solution(9247829643360210313)
XLA Ops:
  0.6 55.4 %shard_map.137 = (bf16[8,1024,128]{2,1,0:T(8,128)(2,1)}, f32[8,128]{1,0:T(8,128)}, bf16[512,128]{1,0:T(8,128)(2,1)}, bf16[512,128]{1,0:T(8,128)(2,1)}) custom-call(bf16[512,1024]{1,0:T(8,128)(2,1)} %feat_ref.1, bf16[512,1024]{1,0:T(8,128)(2,1)} %cot_ref.1, bf16[1024,1024]{1,0:T(8,128)(2,1)} %w_hbm.1, f32[1,1024]{1,0:T(1,128)} %bitcast.9, s32[8,256]{1,0:T(8,128)} %bitcast.7, ...), custom_call_target="tpu_custom_call" | custom-call | tf_op jit(solution)/shard_map/pallas_call | solution.py:434
  56.0 8.7 %shard_map.138 = (f32[1024,1024]{1,0:T(8,128)}, f32[8,128]{1,0:T(8,128)}, bf16[512,128]{1,0:T(8,128)(2,1)}, f32[32,128]{1,0:T(8,128)}, f32[4096,128]{1,0:T(8,128)}) custom-call(bf16[8,1024,128]{2,1,0:T(8,128)(2,1)} %get-tuple-element.14.wsum_ref, f32[8,128]{1,0:T(8,128)} %get-tuple-element.15.bsum_ref, bf16[512,128]{1,0:T(8,128)(2,1)} %get-tuple-element.16.dense_ref, ...), custom_call_target="tpu_custom_call" | custom-call | tf_op jit(solution)/shard_map/pallas_call | solution.py:539

commit v5 on v4

--- a/solution.py
+++ b/solution.py
@@ -82,6 +82,7 @@
     tblk = touched_count // n_rep
     slots = bags_ref.shape[1]
     inverse = (1 << 16) // feats + 1
+    assert n_rep == 4
     assert tok * feats * (inverse * feats - (1 << 16)) < 1 << 16
 
     def rep_peer(o):
@@ -256,13 +257,38 @@
         ]
         return remote(place, place, agz_sem, k * nz + o, {"shard": z_peer(o) * 2 + core})
 
-    def agr(k, o, q):
+    def flip(mask):
+        if mask == 1:
+            return rep + 1 - 2 * lax.rem(rep, 2)
+        return lax.rem(rep + 2, 4) if mask == 2 else 3 - rep
+
+    def owner(k, o):
+        return rep if o == 0 else flip((2 - k % 2, 1 + k % 2, 3)[o - 1])
+
+    def agr(k, o, arriving=False):
+        q = owner(k, o) if arriving else owner(k, 1 if o == 3 else 0)
         place = wsum_ref.at[core * parts + k, rep_rows(q), :]
-        return remote(place, place, agr_sem, k * n_rep + o, {"rep": rep_peer(o)})
-
-    def agc(k, o, q, side):
-        place = wsum_ref.at[side * parts + k, rep_rows(q), :]
+        target = owner(k, 1 if o == 1 else 2)
+        return remote(place, place, agr_sem, k * n_rep + o, {"rep": target})
+
+    def agc(k, o, side):
+        place = wsum_ref.at[side * parts + k, rep_rows(owner(k, o)), :]
         return remote(place, place, agc_sem, k * n_rep + o, {"shard": partner})
+
+    def forward(k):
+        agr(k, 1, True).wait_recv()
+        agr(k, 3).start()
+        agc(k, 1, core).start()
+
+    def write_out(side, k):
+        piece = side * parts + k
+        return pltpu.make_async_copy(wsum_ref.at[piece], wsum_hbm.at[piece], out_sem.at[piece])
+
+    def finish(k):
+        for o in (2, 3):
+            agr(k, o, True).wait_recv()
+            agc(k, o, core).start()
+        write_out(core, k).start()
 
     cuts = (1, n_shard // 2 - 1, n_shard - 2, n_shard)
     for t in range(parts + 2):
@@ -293,9 +319,12 @@
             k = t - 2
             for o in range(1, nz):
                 agz(k, o, z_from(o)).wait_recv()
-            for o in range(1, n_rep):
-                agr(k, o, rep).start()
-            agc(k, 0, rep, core).start()
+            for o in (1, 2):
+                agr(k, o).start()
+            agc(k, 0, core).start()
+
+    for k in range(parts - 1):
+        forward(k)
 
     incoming[shard] = gather(shard)
     dense_ref[...] = ig[:, :width]
@@ -345,15 +374,9 @@
     for o in range(1, n_rep):
         rrs(o).start()
 
-    def write_out(side, k):
-        piece = side * parts + k
-        return pltpu.make_async_copy(wsum_ref.at[piece], wsum_hbm.at[piece], out_sem.at[piece])
-
+    forward(parts - 1)
     for k in range(parts // 2):
-        for o in range(1, n_rep):
-            agr(k, o, rep_from(o)).wait_recv()
-            agc(k, o, rep_from(o), core).start()
-        write_out(core, k).start()
+        finish(k)
 
     for o in range(1, n_rep):
         rrs(o).wait_recv()
@@ -378,15 +401,12 @@
     bsum_ref[...] = bias_all
 
     for k in range(parts // 2, parts):
-        for o in range(1, n_rep):
-            agr(k, o, rep_from(o)).wait_recv()
-            agc(k, o, rep_from(o), core).start()
-        write_out(core, k).start()
+        finish(k)
     for o in range(1, n_rep):
         rag(o, rep_from(o)).wait_recv()
     for k in range(parts):
         for o in range(n_rep):
-            agc(k, o, rep_from(o), 1 - core).wait_recv()
+            agc(k, o, 1 - core).wait_recv()
         write_out(1 - core, k).start()
 
     b1.wait_send()
@@ -400,12 +420,12 @@
         p1(k).wait_send()
         for o in range(1, n_rep):
             p2(k, o).wait_send()
-            agr(k, o, rep).wait_send()
+            agr(k, o).wait_send()
         for o in range(1, nz):
             p3(k, o).wait_send()
             agz(k, o, zi).wait_send()
         for o in range(n_rep):
-            agc(k, o, rep_from(o), core).wait_send()
+            agc(k, o, core).wait_send()
         write_out(core, k).wait()
         write_out(1 - core, k).wait()
 

time: 65 us -> 66.9 us (1.029)
  Pallas kernels: 64.1 us -> 65.9 us
    pallas_call x1, Pallas kernels: 55.4 us -> 57.3 us  [step_call(): pl.pallas_call(functools.partial(step_kernel, n_rep, n_shard), out_shape=...]
where the time goes in v5:
time: 66.9 us; the launch traced here: 66.6 us
  Pallas kernels  65.9 us (99%)
    pallas_call x1, Pallas kernels, step_call(): pl.pallas_call(functools.partial(step_kernel, n_rep, n_shard), out_shape=...  57.3 us
    pallas_call x1, Pallas kernels, update_call(): pl.pallas_call(functools.partial(update_kernel, scale), grid=(steps,), in...  8.67 us

profile of v5, /device:TPU:0, one launch (start us, length us, event | category | flops | bytes accessed | tf_op | source)
XLA Modules:
  0.0 66.6 jit_solution(9332217460905415397)
XLA Ops:
  0.6 57.3 %shard_map.137 = (bf16[8,1024,128]{2,1,0:T(8,128)(2,1)}, f32[8,128]{1,0:T(8,128)}, bf16[512,128]{1,0:T(8,128)(2,1)}, bf16[512,128]{1,0:T(8,128)(2,1)}) custom-call(bf16[512,1024]{1,0:T(8,128)(2,1)} %feat_ref.1, bf16[512,1024]{1,0:T(8,128)(2,1)} %cot_ref.1, bf16[1024,1024]{1,0:T(8,128)(2,1)} %w_hbm.1, f32[1,1024]{1,0:T(1,128)} %bitcast.9, s32[8,256]{1,0:T(8,128)} %bitcast.7, ...), custom_call_target="tpu_custom_call" | custom-call | tf_op jit(solution)/shard_map/pallas_call | solution.py:454
  57.9 8.7 %shard_map.138 = (f32[1024,1024]{1,0:T(8,128)}, f32[8,128]{1,0:T(8,128)}, bf16[512,128]{1,0:T(8,128)(2,1)}, f32[32,128]{1,0:T(8,128)}, f32[4096,128]{1,0:T(8,128)}) custom-call(bf16[8,1024,128]{2,1,0:T(8,128)(2,1)} %get-tuple-element.14.wsum_ref, f32[8,128]{1,0:T(8,128)} %get-tuple-element.15.bsum_ref, bf16[512,128]{1,0:T(8,128)(2,1)} %get-tuple-element.16.dense_ref, ...), custom_call_target="tpu_custom_call" | custom-call | tf_op jit(solution)/shard_map/pallas_call | solution.py:559
